TPU v7x, 512 devices: a whole 4x4x16 slice. The times are simulated.
512 devices in a mesh: domain: 64 (over z_lo, y, core), band: 8 (over x, z_hi).
Axes of the slice: x: 4, y: 4, z: 16 (z_hi: 2, z_lo: 8; z = z_hi * 8 + z_lo), core: 2. Of those that a mesh axis runs over, the one named last changes fastest.
Arguments:
- states: float32 [110592, 1024], P('domain', 'band'), may hold values from -6 to 6
- connectivity: int32 [512, 343], P('domain'), may hold values from 0 to 2303, as said below
- cell_hamiltonian: float32 [512, 343, 343], P(('domain', 'band')), as said below
Outputs:
- filtered: float32 [110592, 1024], P('domain', 'band')
Inputs may be any that keep to these rules, and one draw needn't show every extreme that they name: `connectivity`: each cell names 343 distinct positions of its subdomain's extended list of 2304 nodes. `cell_hamiltonian`: each matrix is symmetric.
All inputs are finite; a program needn't handle non-finite values.
Results may differ from a plain program's by a relative error of at most 0.0001.
Values sent between devices are 32-bit elements; how exact they have to be, the bound alone decides.
A program may use at most 64 MiB of HBM per device.

v0:
```python
import jax
import jax.numpy as jnp
from jax import lax
from jax.sharding import PartitionSpec as P

FACE = 288


filter_center = 0.5
filter_half = 1.5


def extended_2(block, sides, width):
    for axis, dim in sides:
        count = lax.axis_size(axis)
        forward = [(i, i + 1) for i in range(count - 1)]
        backward = [(target, source) for source, target in forward]
        low = lax.ppermute(
            lax.slice_in_dim(block, block.shape[dim] - width, None, axis=dim), axis, forward
        )
        high = lax.ppermute(lax.slice_in_dim(block, 0, width, axis=dim), axis, backward)
        block = jnp.concatenate([low, block, high], axis=dim)
    return block


def passed_along(block, axis, distance):
    devices = range(lax.axis_size(axis))
    route = [(i - distance, i) for i in devices if i - distance in devices]
    return lax.ppermute(block, axis, route)


def apply_cells(total, extended, links, blocks):
    picked = extended[links]
    prods = jnp.einsum("cij,cjs->cis", blocks, picked, precision=lax.Precision.HIGHEST)
    return total.at[links.reshape(-1)].add(prods.reshape(-1, extended.shape[1]))


def operate(field, connectivity, held):
    own_rows = field.shape[0]
    extended = extended_2(field, (("domain", 0),), FACE)
    empty = jnp.zeros(extended.shape, jnp.float32)
    total = apply_cells(
        empty, extended, connectivity, lax.all_gather(held, "band", axis=0, tiled=True)
    )
    owned = total[FACE : FACE + own_rows]
    from_upper = passed_along(total[:FACE], "domain", -1)
    from_lower = passed_along(total[FACE + own_rows :], "domain", 1)
    owned = owned.at[:FACE].add(from_lower)
    owned = owned.at[own_rows - FACE :].add(from_upper)
    return owned


def on_device(states, connectivity, cell_hamiltonian):
    applied = operate(states, connectivity, cell_hamiltonian)
    first = (applied - filter_center * states) / filter_half
    second = operate(first, connectivity, cell_hamiltonian)
    return 2.0 * (second - filter_center * first) / filter_half - states


def solution(mesh):
    return jax.shard_map(
        on_device,
        mesh=mesh,
        in_specs=(P("domain", "band"), P("domain", None), P(("domain", "band"), None, None)),
        out_specs=P("domain", "band"),
        check_vma=False,
    )
```

profile of v0, /device:TPU:25, one launch (start us, length us, event | category | flops | bytes accessed | tf_op | source)
XLA Modules:
  0.0 295.7 jit_solution(8100902115470965008)
XLA Ops:
  6.5 1.9 copy.6
  8.6 3.8 %collective-permute-start = (f32[288,128]{1,0:T(8,128)S(1)}, f32[288,128]{1,0:T(8,128)S(1)}, u32[]{:S(2)}, u32[]{:S(2)}) collective-permute-start(f32[288,128]{1,0:T(8,128)S(1)} %get-tuple-element.59), channel_id=1, source_target_pairs={{0,8},{8,16},{16,24},{24,32},{32,40},{40,48},{48,56},{56,64},{64,7... | collective-permute-start | bytes 442376 | tf_op jit(solution)/shard_map/ppermute | solution.py:18
  12.3 1.9 collective-permute-start.1
  14.5 6.4 %collective-permute-done.1 = f32[288,128]{1,0:T(8,128)S(1)} collective-permute-done((f32[288,128]{1,0:T(8,128)S(1)}, f32[288,128]{1,0:T(8,128)S(1)}, u32[]{:S(2)}, u32[]{:S(2)}) %collective-permute-start.1) | collective-permute-done | bytes 147488 | tf_op jit(solution)/shard_map/ppermute | solution.py:21
  21.0 4.8 %gather_fusion = f32[2744,128]{1,0:T(8,128)S(1)} fusion(f32[2304,128]{1,0:T(8,128)S(1)} %pad_maximum_fusion, s32[3072]{0:T(1024)S(1)} %pad_clamp_fusion), kind=kCustom, calls=%fused_computation | custom fusion | bytes 2820832 | tf_op jit(solution)/shard_map/gather | solution.py:33
  25.8 1.2 reshape.137
  27.0 167.2 %all-gather.2.cloned.1.call-done = f32[8,343,343]{2,1,0:T(8,128)} async-done(((f32[1,343,343]{2,1,0:T(8,128)}), f32[8,343,343]{2,1,0:T(8,128)}) %all-gather.2.cloned.1.call-update) | async-done | bytes 3764784 | tf_op jit(solution)/shard_map/all_gather | solution.py:43
  194.3 7.2 %convolution_bitcast_fusion.1 = f32[8,343,128]{2,1,0:T(8,128)S(1)} fusion(f32[8,343,128]{2,1,0:T(8,128)} %reshape.137, f32[8,343,343]{2,1,0:T(8,128)} %all-gather.2.cloned.1.call-done), kind=kOutput, calls=%fused_computation.5 | convolution fusion | flops 1445670912 | bytes 6574624 | tf_op jit(solution)/shard_map/cij,cjs->cis/dot_general | solution.py:34
  201.5 1.2 reshape.156
  202.7 17.6 %scatter_custom_fusion = f32[2304,128]{1,0:T(8,128)S(1)} fusion(s32[2744]{0:T(1024)S(1)} %fusion.9, f32[2744,128]{1,0:T(8,128)} %reshape.156, f32[]{:T(128)} %constant.106.clone.1), kind=kCustom, calls=%fused_computation.13 | custom fusion | flops 351232 | bytes 1180160 | tf_op jit(solution)/shard_map/scatter-add | solution.py:35
  220.3 1.9 collective-permute-start.2
  222.3 3.0 %collective-permute-start.3 = (f32[288,128]{1,0:T(8,128)S(1)}, f32[288,128]{1,0:T(8,128)S(1)}, u32[]{:S(2)}, u32[]{:S(2)}) collective-permute-start(f32[288,128]{1,0:T(8,128)S(1)} %get-tuple-element.55), channel_id=1, source_target_pairs={{8,0},{16,8},{24,16},{32,24},{40,32},{48,40},{56,48},{64,56},{72,6... | collective-permute-start | bytes 442376 | tf_op jit(solution)/shard_map/ppermute | solution.py:29
  225.3 5.5 %collective-permute-done.3 = f32[288,128]{1,0:T(8,128)S(1)} collective-permute-done((f32[288,128]{1,0:T(8,128)S(1)}, f32[288,128]{1,0:T(8,128)S(1)}, u32[]{:S(2)}, u32[]{:S(2)}) %collective-permute-start.3) | collective-permute-done | bytes 147488 | tf_op jit(solution)/shard_map/ppermute | solution.py:29
  231.1 1.9 collective-permute-start.4
  233.0 2.6 collective-permute-start.5
  235.6 6.0 %collective-permute-done.5 = f32[288,128]{1,0:T(8,128)S(1)} collective-permute-done((f32[288,128]{1,0:T(8,128)S(1)}, f32[288,128]{1,0:T(8,128)S(1)}, u32[]{:S(2)}, u32[]{:S(2)}) %collective-permute-start.5) | collective-permute-done | bytes 147488 | tf_op jit(solution)/shard_map/ppermute | solution.py:21
  241.7 5.9 %gather_fusion.1 = f32[2744,128]{1,0:T(8,128)} fusion(f32[2304,128]{1,0:T(8,128)S(1)} %pad_maximum_fusion.1, s32[3072]{0:T(1024)S(1)} %pad_clamp_fusion), kind=kCustom, calls=%fused_computation.1 | custom fusion | bytes 2820832 | tf_op jit(solution)/shard_map/gather | solution.py:33
  247.6 1.4 reshape.145
  249.0 7.9 %convolution_bitcast_fusion = f32[8,343,128]{2,1,0:T(8,128)} fusion(f32[8,343,128]{2,1,0:T(8,128)S(1)} %reshape.145, f32[8,343,343]{2,1,0:T(8,128)} %all-gather.2.cloned.1.call-done), kind=kOutput, calls=%fused_computation.4 | convolution fusion | flops 1445670912 | bytes 6574624 | tf_op jit(solution)/shard_map/cij,cjs->cis/dot_general | solution.py:34
  256.9 2.5 reshape.164
  259.5 17.6 %scatter_custom_fusion.1 = f32[2304,128]{1,0:T(8,128)S(1)} fusion(s32[2744]{0:T(1024)S(1)} %fusion.9, f32[2744,128]{1,0:T(8,128)} %reshape.164, f32[]{:T(128)} %constant.106.clone.1), kind=kCustom, calls=%fused_computation.11 | custom fusion | flops 351232 | bytes 1180160 | tf_op jit(solution)/shard_map/scatter-add | solution.py:35
  277.1 1.9 collective-permute-start.6
  279.1 2.4 collective-permute-start.7
  281.5 6.1 %collective-permute-done.7 = f32[288,128]{1,0:T(8,128)S(1)} collective-permute-done((f32[288,128]{1,0:T(8,128)S(1)}, f32[288,128]{1,0:T(8,128)S(1)}, u32[]{:S(2)}, u32[]{:S(2)}) %collective-permute-start.7) | collective-permute-done | bytes 147488 | tf_op jit(solution)/shard_map/ppermute | solution.py:29
  (29 shorter events, 2.0 us)
Async XLA Ops:
  6.5 2.0 copy-start
  6.5 7.7 %copy-start.1 = (s32[8,343]{1,0:T(8,128)S(1)}, s32[8,343]{1,0:T(8,128)}, u32[]{:S(2)}) copy-start(s32[8,343]{1,0:T(8,128)} %param.12) | copy-start | bytes 32932
  6.5 187.7 %all-gather.2.cloned.1.call-start = ((), (), s32[]{:S(2)}) async-start(), calls=%async_computation | async-start | bytes 4755456 | tf_op jit(solution)/shard_map/all_gather | solution.py:43
  8.6 6.0 %collective-permute-start = (f32[288,128]{1,0:T(8,128)S(1)}, f32[288,128]{1,0:T(8,128)S(1)}, u32[]{:S(2)}, u32[]{:S(2)}) collective-permute-start(f32[288,128]{1,0:T(8,128)S(1)} %get-tuple-element.59), channel_id=1, source_target_pairs={{0,8},{8,16},{16,24},{24,32},{32,40},{40,48},{48,56},{56,64},{64,7... | collective-permute-start | bytes 442376 | tf_op jit(solution)/shard_map/ppermute | solution.py:18
  12.3 8.6 %collective-permute-start.1 = (f32[288,128]{1,0:T(8,128)S(1)}, f32[288,128]{1,0:T(8,128)S(1)}, u32[]{:S(2)}, u32[]{:S(2)}) collective-permute-start(f32[288,128]{1,0:T(8,128)S(1)} %get-tuple-element.60), channel_id=1, source_target_pairs={{8,0},{16,8},{24,16},{32,24},{40,32},{48,40},{56,48},{64,56},{72,6... | collective-permute-start | bytes 442376 | tf_op jit(solution)/shard_map/ppermute | solution.py:21
  220.3 5.0 %collective-permute-start.2 = (f32[288,128]{1,0:T(8,128)S(1)}, f32[288,128]{1,0:T(8,128)S(1)}, u32[]{:S(2)}, u32[]{:S(2)}) collective-permute-start(f32[288,128]{1,0:T(8,128)S(1)} %get-tuple-element.56), channel_id=1, source_target_pairs={{0,8},{8,16},{16,24},{24,32},{32,40},{40,48},{48,56},{56,64},{64,7... | collective-permute-start | bytes 442376 | tf_op jit(solution)/shard_map/ppermute | solution.py:29
  222.3 8.6 %collective-permute-start.3 = (f32[288,128]{1,0:T(8,128)S(1)}, f32[288,128]{1,0:T(8,128)S(1)}, u32[]{:S(2)}, u32[]{:S(2)}) collective-permute-start(f32[288,128]{1,0:T(8,128)S(1)} %get-tuple-element.55), channel_id=1, source_target_pairs={{8,0},{16,8},{24,16},{32,24},{40,32},{48,40},{56,48},{64,56},{72,6... | collective-permute-start | bytes 442376 | tf_op jit(solution)/shard_map/ppermute | solution.py:29
  231.1 4.5 %collective-permute-start.4 = (f32[288,128]{1,0:T(8,128)S(1)}, f32[288,128]{1,0:T(8,128)S(1)}, u32[]{:S(2)}, u32[]{:S(2)}) collective-permute-start(f32[288,128]{1,0:T(8,128)S(1)} %get-tuple-element.57), channel_id=1, source_target_pairs={{0,8},{8,16},{16,24},{24,32},{32,40},{40,48},{48,56},{56,64},{64,7... | collective-permute-start | bytes 442376 | tf_op jit(solution)/shard_map/ppermute | solution.py:18
  233.0 8.6 %collective-permute-start.5 = (f32[288,128]{1,0:T(8,128)S(1)}, f32[288,128]{1,0:T(8,128)S(1)}, u32[]{:S(2)}, u32[]{:S(2)}) collective-permute-start(f32[288,128]{1,0:T(8,128)S(1)} %get-tuple-element.58), channel_id=1, source_target_pairs={{8,0},{16,8},{24,16},{32,24},{40,32},{48,40},{56,48},{64,56},{72,6... | collective-permute-start | bytes 442376 | tf_op jit(solution)/shard_map/ppermute | solution.py:21
  277.1 4.4 %collective-permute-start.6 = (f32[288,128]{1,0:T(8,128)S(1)}, f32[288,128]{1,0:T(8,128)S(1)}, u32[]{:S(2)}, u32[]{:S(2)}) collective-permute-start(f32[288,128]{1,0:T(8,128)S(1)} %get-tuple-element.54), channel_id=1, source_target_pairs={{0,8},{8,16},{16,24},{24,32},{32,40},{40,48},{48,56},{56,64},{64,7... | collective-permute-start | bytes 442376 | tf_op jit(solution)/shard_map/ppermute | solution.py:29
  279.1 8.6 %collective-permute-start.7 = (f32[288,128]{1,0:T(8,128)S(1)}, f32[288,128]{1,0:T(8,128)S(1)}, u32[]{:S(2)}, u32[]{:S(2)}) collective-permute-start(f32[288,128]{1,0:T(8,128)S(1)} %get-tuple-element.53), channel_id=1, source_target_pairs={{8,0},{16,8},{24,16},{32,24},{40,32},{48,40},{56,48},{64,56},{72,6... | collective-permute-start | bytes 442376 | tf_op jit(solution)/shard_map/ppermute | solution.py:29
Sparse Core Ops, SparseCore 0:
  10.6 183.6 all-gather.1
where the time goes:
time: 297 us; the launch traced here: 296 us
  waiting for transfers between devices  191 us (64%)
  other arithmetic  36.7 us (12%)
  local copies, waits for them, and re-layouts  19.5 us (7%)
  starting transfers between devices  19.4 us (7%)
  matrix products  15.1 us (5%)
  between operations  13.7 us (5%)
    all_gather x1, waiting for transfers between devices, operate(): lax.all_gather(held, 'band', axis=0, tiled=True)  167 us
    scatter-add x2, other arithmetic, apply_cells(): return total.at[links.reshape(-1)].add(prods.reshape(-1, extended.shape[1]))  35.2 us
    dot_general x2, matrix products, apply_cells(): jnp.einsum('cij,cjs->cis', blocks, picked, precision=lax.Precision.HIGHEST)  15.1 us
    gather x4, local copies, waits for them, and re-layouts, apply_cells(): picked = extended[links]  13.4 us
    ppermute x2, waiting for transfers between devices, extended_2(): lax.ppermute(lax.slice_in_dim(block, 0, width, axis=dim), axis, backward)  12.3 us
    ppermute x4, waiting for transfers between devices, passed_along(): return lax.ppermute(block, axis, route)  11.7 us
    ppermute x4, starting transfers between devices, passed_along(): return lax.ppermute(block, axis, route)  9.23 us
  transfers between devices with their start and end apart: 9, of which 5 were waited for; matrix products, arithmetic and copies ran while one was open for 2% of the time, Pallas kernels for 0%

commit v1 on v0

v1 whole, which is shorter than its diff:
```python
import functools

import jax
import jax.numpy as jnp
from jax import lax
from jax.experimental import pallas as pl
from jax.experimental.pallas import tpu as pltpu
from jax.sharding import PartitionSpec as P

MESH = pl.DeviceIdType.MESH
f32, bf16, i32, i16 = jnp.float32, jnp.bfloat16, jnp.int32, jnp.int16

NPC = 343
KC = 352
CELLS = 8
FACE = 288
OWN = 1728
EXT = OWN + 2 * FACE
COLS = 128
INNER = OWN - 2 * FACE

LOW = INNER
HIGH = INNER + 2 * FACE
EARLY = 1024

PB, PA, PD, PC, PROWS = 0, 176, 304, 432, 520
PIECES = ((PB, 176), (PA, 128), (PD, 128), (PC, 88))

center = 0.5
half = 1.5


def split(value):
    hi = value.astype(bf16)
    lo = (value - hi.astype(f32)).astype(bf16)
    return hi, lo


def kernel(
    states, conn, cell, out,
    G, S, Hs, X, PR, E, RX, T, SX, F, XR, YR, Hf, CP, CR,
    z_send, x_send, f_send, n_send, cell_recv, n_recv,
):
    d = lax.axis_index("domain")
    b = lax.axis_index("band")
    last = lax.axis_size("domain") - 1
    nx = CELLS // 2
    xi = b // 2
    zh = b % 2
    zpeer = 2 * xi + 1 - zh
    xpeers = [2 * ((xi + j) % nx) + zh for j in (1, 3, 2)]
    has_low = d > 0
    has_high = d < last

    barrier = pltpu.get_barrier_semaphore()

    def greet(dd, bb):
        pl.semaphore_signal(barrier, inc=1, device_id=(dd, bb), device_id_type=MESH)

    greet(d, zpeer)
    for p in xpeers:
        greet(d, p)

    @pl.when(has_low)
    def _():
        greet(d - 1, b)

    @pl.when(has_high)
    def _():
        greet(d + 1, b)

    Hf[...] = jnp.zeros_like(Hf)
    Hf[0:NPC, 0:NPC] = cell[0]
    row = lax.broadcasted_iota(i32, (128, 128), 0)
    col = lax.broadcasted_iota(i32, (128, 128), 1)
    row88 = lax.broadcasted_iota(i32, (88, 128), 0)
    d2 = Hf[128:256, 128:256]
    diag = jnp.sum(jnp.where(row == col, d2, 0.0), axis=0, keepdims=True)
    RX[b, PB : PB + 88] = jnp.where(row88 == 87, diag, Hf[256:344, 0:128])
    RX[b, PB + 88 : PB + 176] = Hf[256:344, 128:256]
    RX[b, PA : PA + 128] = Hf[128:256, 0:128]
    RX[b, PD : PD + 128] = jnp.where(row >= col, Hf[0:128, 0:128], d2)
    RX[b, PC : PC + 88] = Hf[256:344, 256:384]

    pl.semaphore_wait(barrier, 4 + has_low.astype(i32) + has_high.astype(i32))

    def piece_copy(e, k, target, send_sem):
        at, rows = PIECES[k]
        part = RX.at[e, pl.ds(at, rows)]
        return pltpu.make_async_remote_copy(
            src_ref=part, dst_ref=part, send_sem=send_sem, recv_sem=cell_recv.at[e, k],
            device_id=(d, target), device_id_type=MESH,
        )

    def whole_copy(e, target, send_sem):
        return pltpu.make_async_remote_copy(
            src_ref=RX.at[e], dst_ref=RX.at[e], send_sem=send_sem, recv_sem=cell_recv.at[e, 0],
            device_id=(d, target), device_id_type=MESH,
        )

    def node_copy(src, dst, i, dd):
        return pltpu.make_async_remote_copy(
            src_ref=src, dst_ref=dst, send_sem=n_send.at[i], recv_sem=n_recv.at[i],
            device_id=(dd, b), device_id_type=MESH,
        )

    z_copies = [piece_copy(b, k, zpeer, z_send.at[k]) for k in range(4)]
    for c in z_copies:
        c.start()
    x_copies = [whole_copy(b, p, x_send.at[j]) for j, p in enumerate(xpeers)]
    for c in x_copies:
        c.start()

    def exchange(step, down_src, down_dst, up_src, up_dst):
        down = node_copy(down_src, down_dst, 2 * step, d - 1)
        up = node_copy(up_src, up_dst, 2 * step + 1, d + 1)
        return down, up

    halo_down, halo_up = exchange(
        0, states.at[pl.ds(0, FACE)], SX.at[pl.ds(HIGH + FACE, FACE)],
        states.at[pl.ds(OWN - FACE, FACE)], SX.at[pl.ds(LOW, FACE)],
    )
    sum_down, sum_up = exchange(
        1, T.at[pl.ds(LOW, 2 * FACE)], XR.at[1], T.at[pl.ds(HIGH, 2 * FACE)], XR.at[0]
    )
    own_down, own_up = exchange(
        2, T.at[pl.ds(LOW, FACE)], YR.at[1], T.at[pl.ds(HIGH + FACE, FACE)], YR.at[0]
    )

    @pl.when(has_low)
    def _():
        halo_down.start()

    @pl.when(has_high)
    def _():
        halo_up.start()

    CP[...] = jnp.full(CP.shape, -1, i32)
    n = conn[...]
    CP[:, 0:NPC] = jnp.where(n < 2 * FACE, n + LOW, jnp.where(n < OWN, n - 2 * FACE, n))

    def cell_of(s):
        side = s // nx
        return 2 * ((xi + s) % nx) + zh + side * (1 - 2 * zh)

    rows = [CP[pl.ds(cell_of(s), 1), :] for s in range(CELLS)]
    near = [r[:, :KC] for r in rows[:nx]]
    top = [r[:, :256] for r in rows[nx:]]
    bottom = [r[:, 256:KC] for r in rows[nx:]]
    CR[...] = jnp.concatenate(near + top + bottom, axis=1)

    def build_g(s, carry):
        line = jnp.broadcast_to(CP[pl.ds(cell_of(s), 1), :], (8, 384))
        column = jnp.transpose(line)[:KC, 0:1]
        wanted = jnp.broadcast_to(column, (KC, 128)).astype(i16)
        for j in range(EXT // 128):
            place = (lax.broadcasted_iota(i32, (KC, 128), 1) + j * 128).astype(i16)
            G[pl.ds(pl.multiple_of(s * KC, KC), KC), j * 128 : (j + 1) * 128] = jnp.where(
                wanted == place, bf16(1), bf16(0)
            )
        return carry

    lax.fori_loop(0, CELLS, build_g, 0)

    def build_s(j, carry):
        place = (lax.broadcasted_iota(i32, (256, 128), 0) + j * 256).astype(i16)
        for t in range(CELLS * KC // 128):
            wanted = jnp.broadcast_to(CR[0:1, t * 128 : (t + 1) * 128], (256, 128)).astype(i16)
            S[pl.ds(pl.multiple_of(j * 256, 256), 256), t * 128 : (t + 1) * 128] = jnp.where(
                wanted == place, bf16(1), bf16(0)
            )
        return carry

    lax.fori_loop(0, EXT // 256, build_s, 0)

    SX[0:INNER] = states[FACE : OWN - FACE]
    SX[LOW + FACE : HIGH] = states[0:FACE]
    SX[HIGH : HIGH + FACE] = states[OWN - FACE : OWN]

    @pl.when(has_low)
    def _():
        halo_up.wait_recv()

    @pl.when(jnp.logical_not(has_low))
    def _():
        SX[LOW : LOW + FACE] = jnp.zeros((FACE, COLS), f32)

    @pl.when(has_high)
    def _():
        halo_down.wait_recv()

    @pl.when(jnp.logical_not(has_high))
    def _():
        SX[HIGH + FACE : EXT] = jnp.zeros((FACE, COLS), f32)

    def set_field(at, count, value):
        hi, lo = split(value)
        E[at : at + count, 0:COLS] = hi
        E[at : at + count, COLS : 2 * COLS] = lo

    set_field(0, EXT, SX[...])

    half_rows = CELLS * KC // 2

    def gather(start, stop, first):
        def body(m, carry):
            r = pl.ds(pl.multiple_of(m * half_rows, half_rows), half_rows)
            got = jnp.dot(G[r, start:stop], E[start:stop], preferred_element_type=f32)
            if not first:
                got = got + X[r, :].astype(f32)
            X[r, :] = got.astype(bf16)
            return carry

        lax.fori_loop(0, 2, body, 0)

    gather(0, EXT, True)

    def forward(k):
        piece_copy(zpeer, k, zpeer, z_send.at[k]).wait_recv()
        for j, p in enumerate(xpeers):
            piece_copy(zpeer, k, p, f_send.at[k, j]).start()

    def put(s, at, count, lane, value):
        hi, lo = split(value)
        base, step = (at, 256) if at < 256 else (512 + at - 256, 96)
        Hs[s, base : base + count, lane : lane + 128] = hi
        Hs[s, base + step : base + step + count, lane : lane + 128] = lo

    def padded(value, count):
        return jnp.concatenate([value, jnp.zeros((count - value.shape[0], 128), f32)], axis=0)

    def unpack_b(s, e):
        for i in range(2):
            part = RX[e, PB + 88 * i : PB + 88 * (i + 1)]
            if i == 0:
                part = jnp.where(row88 == 87, 0.0, part)
            put(s, 256, 96, 128 * i, padded(part, 96))
            put(s, 128 * i, 128, 256, jnp.transpose(padded(part, 128)))

    def unpack_a(s, e):
        part = RX[e, PA : PA + 128]
        put(s, 128, 128, 0, part)
        put(s, 0, 128, 128, jnp.transpose(part))

    def unpack_d(s, e):
        part = RX[e, PD : PD + 128]
        flipped = jnp.transpose(part)
        middle = RX[e, PB + 87 : PB + 88]
        put(s, 0, 128, 0, jnp.where(row >= col, part, flipped))
        put(s, 128, 128, 128, jnp.where(row < col, part, jnp.where(row > col, flipped, middle)))

    def unpack_c(s, e):
        put(s, 256, 96, 256, padded(RX[e, PC : PC + 88], 96))

    def product(s, base, count, at):
        r = pl.ds(pl.multiple_of(s * KC, KC), KC)
        t = jnp.dot(Hs[s, base : base + 2 * count, :KC], X[r, :], preferred_element_type=f32)
        p = (t[count:, COLS:] + t[count:, :COLS]) + (t[:count, COLS:] + t[:count, :COLS])
        hi, lo = split(p)
        w = pl.ds(at, count)
        PR[w, 0:COLS] = hi
        PR[w, COLS : 2 * COLS] = lo

    def top_rows(s, at):
        product(s, 0, 256, at)

    def bottom_rows(s, at):
        product(s, 512, 96, at)

    TOPS = nx * KC
    BOTTOMS = TOPS + nx * 256

    def near_products(j):
        top_rows(j, pl.multiple_of(j * KC, 32))
        bottom_rows(j, pl.multiple_of(j * KC + 256, 32))

    def far_tops(j):
        top_rows(nx + j, pl.multiple_of(TOPS + j * 256, 128))

    def far_bottoms(j):
        bottom_rows(nx + j, pl.multiple_of(BOTTOMS + j * 96, 32))

    def scatter(at, count, start, stop, first):
        got = jnp.dot(S[at : at + count, start:stop], PR[start:stop], preferred_element_type=f32)
        got = got[:, :COLS] + got[:, COLS:]
        T[at : at + count] = got if first else T[at : at + count] + got

    def near_cell(j, carry):
        e = cell_of(j)

        @pl.when(j > 0)
        def _():
            whole_copy(e, zpeer, x_send.at[0]).wait_recv()

        unpack_b(j, e)
        unpack_a(j, e)
        unpack_d(j, e)
        unpack_c(j, e)
        near_products(j)
        return carry

    forward(0)
    lax.fori_loop(0, 2, near_cell, 0)
    forward(1)
    lax.fori_loop(2, nx, near_cell, 0)
    for at in range(0, EXT, EXT // 2):
        scatter(at, EXT // 2, 0, TOPS, True)

    def far(k, unpack):
        def body(j, carry):
            e = cell_of(nx + j)

            @pl.when(j > 0)
            def _():
                piece_copy(e, k, zpeer, z_send.at[k]).wait_recv()

            unpack(nx + j, e)
            return carry

        lax.fori_loop(0, nx, body, 0)

    far(0, unpack_b)
    far(1, unpack_a)
    forward(2)
    forward(3)
    far(2, unpack_d)

    def all_far(rows_of):
        def body(j, carry):
            rows_of(j)
            return carry

        lax.fori_loop(0, nx, body, 0)

    all_far(far_tops)
    for at in range(0, EXT, EXT // 2):
        scatter(at, EXT // 2, TOPS, BOTTOMS, False)
    far(3, unpack_c)
    all_far(far_bottoms)
    end = BOTTOMS + nx * 96
    scatter(LOW, 2 * FACE, BOTTOMS, end, False)

    @pl.when(has_low)
    def _():
        sum_down.start()

    scatter(HIGH, 2 * FACE, BOTTOMS, end, False)

    @pl.when(has_high)
    def _():
        sum_up.start()

    scatter(0, INNER, BOTTOMS, end, False)

    def set_first(at, count, total, keep=None):
        value = (total - center * SX[at : at + count]) * (1.0 / half)
        if keep is not None:
            value = jnp.where(keep, value, 0.0)
        F[at : at + count] = value
        set_field(at, count, value)

    set_first(0, INNER, T[0:INNER])
    gather(0, EARLY, True)

    @pl.when(has_low)
    def _():
        sum_up.wait_recv()

    @pl.when(jnp.logical_not(has_low))
    def _():
        XR[0] = jnp.zeros((2 * FACE, COLS), f32)

    @pl.when(has_high)
    def _():
        sum_down.wait_recv()

    @pl.when(jnp.logical_not(has_high))
    def _():
        XR[1] = jnp.zeros((2 * FACE, COLS), f32)

    set_first(LOW, FACE, T[LOW : LOW + FACE] + XR[0, 0:FACE], has_low)
    set_first(LOW + FACE, FACE, T[LOW + FACE : HIGH] + XR[0, FACE:])
    set_first(HIGH, FACE, T[HIGH : HIGH + FACE] + XR[1, 0:FACE])
    set_first(HIGH + FACE, FACE, T[HIGH + FACE : EXT] + XR[1, FACE:], has_high)
    gather(EARLY, EXT, False)

    def second_near(j, carry):
        near_products(j)
        return carry

    lax.fori_loop(0, nx, second_near, 0)

    def second_far(j, carry):
        far_tops(j)
        far_bottoms(j)
        return carry

    lax.fori_loop(0, nx, second_far, 0)

    @pl.when(has_low)
    def _():
        sum_down.wait_send()

    @pl.when(has_high)
    def _():
        sum_up.wait_send()

    scatter(LOW, FACE, 0, end, True)

    @pl.when(has_low)
    def _():
        own_down.start()

    scatter(HIGH + FACE, FACE, 0, end, True)

    @pl.when(has_high)
    def _():
        own_up.start()

    def finish(to, at, count, total):
        value = (total - center * F[at : at + count]) * (2.0 / half)
        out[to : to + count] = value - SX[at : at + count]

    scatter(0, INNER, 0, end, True)
    finish(FACE, 0, INNER, T[0:INNER])
    scatter(LOW + FACE, 2 * FACE, 0, end, True)

    @pl.when(has_low)
    def _():
        own_up.wait_recv()

    @pl.when(jnp.logical_not(has_low))
    def _():
        YR[0] = jnp.zeros((FACE, COLS), f32)

    @pl.when(has_high)
    def _():
        own_down.wait_recv()

    @pl.when(jnp.logical_not(has_high))
    def _():
        YR[1] = jnp.zeros((FACE, COLS), f32)

    finish(0, LOW + FACE, FACE, T[LOW + FACE : HIGH] + YR[0])
    finish(OWN - FACE, HIGH, FACE, T[HIGH : HIGH + FACE] + YR[1])

    for c in z_copies + x_copies:
        c.wait_send()
    for k in range(4):
        for j, p in enumerate(xpeers):
            piece_copy(zpeer, k, p, f_send.at[k, j]).wait_send()

    @pl.when(has_low)
    def _():
        halo_down.wait_send()
        own_down.wait_send()

    @pl.when(has_high)
    def _():
        halo_up.wait_send()
        own_up.wait_send()


def on_device(states, connectivity, cell_hamiltonian):
    vmem = pl.BlockSpec(memory_space=pltpu.VMEM)
    kt = CELLS * KC
    return pl.pallas_call(
        kernel,
        out_shape=jax.ShapeDtypeStruct((OWN, COLS), f32),
        in_specs=[vmem] * 3,
        out_specs=vmem,
        scratch_shapes=[
            pltpu.VMEM((kt, EXT), bf16),
            pltpu.VMEM((EXT, kt), bf16),
            pltpu.VMEM((CELLS, 2 * KC, 384), bf16),
            pltpu.VMEM((kt, 2 * COLS), bf16),
            pltpu.VMEM((kt, 2 * COLS), bf16),
            pltpu.VMEM((EXT, 2 * COLS), bf16),
            pltpu.VMEM((CELLS, PROWS, 128), f32),
            pltpu.VMEM((EXT, COLS), f32),
            pltpu.VMEM((EXT, COLS), f32),
            pltpu.VMEM((EXT, COLS), f32),
            pltpu.VMEM((2, 2 * FACE, COLS), f32),
            pltpu.VMEM((2, FACE, COLS), f32),
            pltpu.VMEM((KC, 384), f32),
            pltpu.VMEM((CELLS, 384), i32),
            pltpu.VMEM((1, kt), i32),
            pltpu.SemaphoreType.DMA((4,)),
            pltpu.SemaphoreType.DMA((3,)),
            pltpu.SemaphoreType.DMA((4, 3)),
            pltpu.SemaphoreType.DMA((6,)),
            pltpu.SemaphoreType.DMA((CELLS, 4)),
            pltpu.SemaphoreType.DMA((6,)),
        ],
        compiler_params=pltpu.CompilerParams(
            collective_id=0, has_side_effects=True, vmem_limit_bytes=58 << 20
        ),
    )(states, connectivity, cell_hamiltonian)


def solution(mesh):
    return jax.shard_map(
        on_device,
        mesh=mesh,
        in_specs=(P("domain", "band"), P("domain", None), P(("domain", "band"), None, None)),
        out_specs=P("domain", "band"),
        check_vma=False,
    )
```

time: 297 us -> 86.4 us (0.29)
  the two profiles are of different devices: /device:TPU:25 before, /device:TPU:32 now
where the time goes in v1:
time: 86.4 us; the launch traced here: 86.2 us
  Pallas kernels  82.1 us (95%)
  local copies, waits for them, and re-layouts  4.01 us (5%)
    pallas_call x1, Pallas kernels, on_device(): pl.pallas_call(kernel, out_shape=jax.ShapeDtypeStruct((OWN, COLS), f32),...  82.1 us
    unnamed x2, local copies, waits for them, and re-layouts  4.01 us

profile of v1, /device:TPU:32, one launch (start us, length us, event | category | flops | bytes accessed | tf_op | source)
XLA Modules:
  0.0 86.2 jit_solution(785534903563541603)
XLA Ops:
  0.0 1.9 %copy.4.cell = f32[1,343,343]{2,1,0:T(8,128)} copy(f32[1,343,343]{2,0,1:T(1,128)} %param.5) | data formatting | bytes 941192 | tf_op args[2]
  1.9 82.1 %shard_map.37 = f32[1728,128]{1,0:T(8,128)} custom-call(f32[1728,128]{1,0:T(8,128)} %states.1, s32[8,343]{1,0:T(8,128)} %conn.1, f32[1,343,343]{2,1,0:T(8,128)} %copy.4.cell), custom_call_target="tpu_custom_call" | custom-call | tf_op jit(solution)/shard_map/pallas_call | solution.py:467
  84.0 2.1 %copy.6 = f32[1728,128]{1,0:T(8,128)} copy(f32[1728,128]{1,0:T(8,128)} %shard_map.37) | data formatting | bytes 1769472

commit v2 on v1

--- a/solution.py
+++ b/solution.py
@@ -23,8 +23,8 @@
 HIGH = INNER + 2 * FACE
 EARLY = 1024
 
-PB, PA, PD, PC, PROWS = 0, 176, 304, 432, 520
-PIECES = ((PB, 176), (PA, 128), (PD, 128), (PC, 88))
+PB, PA, PD, PC, PROWS = 0, 176, 304, 432, 480
+PIECES = ((PB, 176), (PA, 128), (PD, 128), (PC, 48))
 
 center = 0.5
 half = 1.5
@@ -36,10 +36,44 @@
     return hi, lo
 
 
+def rows_cols(rows):
+    return lax.broadcasted_iota(i32, (rows, 128), 0), lax.broadcasted_iota(i32, (rows, 128), 1)
+
+
+def padded(value, count):
+    return jnp.concatenate([value, jnp.zeros((count - value.shape[0], 128), f32)], axis=0)
+
+
+def pack_corner(corner, roll):
+    row, col = rows_cols(48)
+    second = padded(roll(corner[48:88], 80), 48)
+    both = jnp.where(row >= col, corner[0:48], second)
+    diag = jnp.sum(jnp.where(row == col, second, 0.0), axis=1, keepdims=True)
+    below = padded(corner[48:88], 48)
+    packed = jnp.where(col < 48, below, jnp.where((col >= 64) & (col < 112), roll(both, 64), 0.0))
+    return jnp.where(col == 127, diag, packed)
+
+
+def unpack_corner(packed, roll):
+    row, col = rows_cols(48)
+    flipped = jnp.transpose(padded(packed, 128))
+    both = roll(packed, 64)
+    both_t = flipped[64:112]
+    first = jnp.where(row >= col, both, both_t)
+    second = jnp.where(row < col, both, jnp.where(row > col, both_t, packed[:, 127:128]))
+    upper = jnp.where(col < 48, first, jnp.where(col < 88, roll(flipped[0:48], 48), 0.0))
+    lower = jnp.where(col < 48, packed, jnp.where(col < 88, roll(second, 48), 0.0))
+    return jnp.concatenate([upper, lower[0:40]], axis=0)
+
+
+def lane_roll(value, shift):
+    return pltpu.roll(value, shift, 1)
+
+
 def kernel(
     states, conn, cell, out,
-    G, S, Hs, X, PR, E, RX, T, SX, F, XR, YR, Hf, CP, CR,
-    z_send, x_send, f_send, n_send, cell_recv, n_recv,
+    G, S, Hs, X, PR, E, RX, T, SX, F, XR, YR, Hf, CP, CR, CN, V, O,
+    z_send, x_send, f_send, n_send, cell_recv, n_recv, local,
 ):
     d = lax.axis_index("domain")
     b = lax.axis_index("band")
@@ -69,18 +103,29 @@
     def _():
         greet(d + 1, b)
 
+    load_cell = pltpu.make_async_copy(cell, V, local.at[0])
+    load_conn = pltpu.make_async_copy(conn, CN, local.at[1])
+    loads = [
+        pltpu.make_async_copy(states.at[pl.ds(a, c)], SX.at[pl.ds(to, c)], local.at[2 + i])
+        for i, (a, c, to) in enumerate(
+            ((0, FACE, LOW + FACE), (OWN - FACE, FACE, HIGH), (FACE, INNER, 0))
+        )
+    ]
+    for c in [load_cell, load_conn] + loads:
+        c.start()
+
     Hf[...] = jnp.zeros_like(Hf)
-    Hf[0:NPC, 0:NPC] = cell[0]
-    row = lax.broadcasted_iota(i32, (128, 128), 0)
-    col = lax.broadcasted_iota(i32, (128, 128), 1)
-    row88 = lax.broadcasted_iota(i32, (88, 128), 0)
+    load_cell.wait()
+    Hf[0:NPC, 0:NPC] = V[:, 0, :]
+    row, col = rows_cols(128)
+    row88 = rows_cols(88)[0]
     d2 = Hf[128:256, 128:256]
     diag = jnp.sum(jnp.where(row == col, d2, 0.0), axis=0, keepdims=True)
     RX[b, PB : PB + 88] = jnp.where(row88 == 87, diag, Hf[256:344, 0:128])
     RX[b, PB + 88 : PB + 176] = Hf[256:344, 128:256]
     RX[b, PA : PA + 128] = Hf[128:256, 0:128]
     RX[b, PD : PD + 128] = jnp.where(row >= col, Hf[0:128, 0:128], d2)
-    RX[b, PC : PC + 88] = Hf[256:344, 256:384]
+    RX[b, PC : PC + 48] = pack_corner(Hf[256:344, 256:384], lane_roll)
 
     pl.semaphore_wait(barrier, 4 + has_low.astype(i32) + has_high.astype(i32))
 
@@ -117,8 +162,8 @@
         return down, up
 
     halo_down, halo_up = exchange(
-        0, states.at[pl.ds(0, FACE)], SX.at[pl.ds(HIGH + FACE, FACE)],
-        states.at[pl.ds(OWN - FACE, FACE)], SX.at[pl.ds(LOW, FACE)],
+        0, SX.at[pl.ds(LOW + FACE, FACE)], SX.at[pl.ds(HIGH + FACE, FACE)],
+        SX.at[pl.ds(HIGH, FACE)], SX.at[pl.ds(LOW, FACE)],
     )
     sum_down, sum_up = exchange(
         1, T.at[pl.ds(LOW, 2 * FACE)], XR.at[1], T.at[pl.ds(HIGH, 2 * FACE)], XR.at[0]
@@ -127,6 +172,9 @@
         2, T.at[pl.ds(LOW, FACE)], YR.at[1], T.at[pl.ds(HIGH + FACE, FACE)], YR.at[0]
     )
 
+    loads[0].wait()
+    loads[1].wait()
+
     @pl.when(has_low)
     def _():
         halo_down.start()
@@ -136,7 +184,8 @@
         halo_up.start()
 
     CP[...] = jnp.full(CP.shape, -1, i32)
-    n = conn[...]
+    load_conn.wait()
+    n = CN[...]
     CP[:, 0:NPC] = jnp.where(n < 2 * FACE, n + LOW, jnp.where(n < OWN, n - 2 * FACE, n))
 
     def cell_of(s):
@@ -173,9 +222,7 @@
 
     lax.fori_loop(0, EXT // 256, build_s, 0)
 
-    SX[0:INNER] = states[FACE : OWN - FACE]
-    SX[LOW + FACE : HIGH] = states[0:FACE]
-    SX[HIGH : HIGH + FACE] = states[OWN - FACE : OWN]
+    loads[2].wait()
 
     @pl.when(has_low)
     def _():
@@ -226,9 +273,6 @@
         Hs[s, base : base + count, lane : lane + 128] = hi
         Hs[s, base + step : base + step + count, lane : lane + 128] = lo
 
-    def padded(value, count):
-        return jnp.concatenate([value, jnp.zeros((count - value.shape[0], 128), f32)], axis=0)
-
     def unpack_b(s, e):
         for i in range(2):
             part = RX[e, PB + 88 * i : PB + 88 * (i + 1)]
@@ -250,35 +294,37 @@
         put(s, 128, 128, 128, jnp.where(row < col, part, jnp.where(row > col, flipped, middle)))
 
     def unpack_c(s, e):
-        put(s, 256, 96, 256, padded(RX[e, PC : PC + 88], 96))
-
-    def product(s, base, count, at):
-        r = pl.ds(pl.multiple_of(s * KC, KC), KC)
-        t = jnp.dot(Hs[s, base : base + 2 * count, :KC], X[r, :], preferred_element_type=f32)
-        p = (t[count:, COLS:] + t[count:, :COLS]) + (t[:count, COLS:] + t[:count, :COLS])
-        hi, lo = split(p)
-        w = pl.ds(at, count)
-        PR[w, 0:COLS] = hi
-        PR[w, COLS : 2 * COLS] = lo
-
-    def top_rows(s, at):
-        product(s, 0, 256, at)
-
-    def bottom_rows(s, at):
-        product(s, 512, 96, at)
+        put(s, 256, 96, 256, padded(unpack_corner(RX[e, PC : PC + 48], lane_roll), 96))
 
     TOPS = nx * KC
     BOTTOMS = TOPS + nx * 256
 
-    def near_products(j):
-        top_rows(j, pl.multiple_of(j * KC, 32))
-        bottom_rows(j, pl.multiple_of(j * KC + 256, 32))
-
-    def far_tops(j):
-        top_rows(nx + j, pl.multiple_of(TOPS + j * 256, 128))
-
-    def far_bottoms(j):
-        bottom_rows(nx + j, pl.multiple_of(BOTTOMS + j * 96, 32))
+    def product(s, base, count, *parts):
+        t = jnp.dot(
+            Hs[s, base : base + count, :KC], X[s * KC : (s + 1) * KC], preferred_element_type=f32
+        )
+        for at, rows, to in parts:
+            hi_part, lo_part = t[at : at + rows], t[at + rows : at + 2 * rows]
+            p = (lo_part[:, COLS:] + lo_part[:, :COLS]) + (hi_part[:, COLS:] + hi_part[:, :COLS])
+            hi, lo = split(p)
+            PR[to : to + rows, 0:COLS] = hi
+            PR[to : to + rows, COLS : 2 * COLS] = lo
+
+    def near_products():
+        for j in range(nx):
+            product(j, 0, 704, (0, 256, j * KC), (512, 96, j * KC + 256))
+
+    def far_tops():
+        for j in range(nx):
+            product(nx + j, 0, 512, (0, 256, TOPS + j * 256))
+
+    def far_bottoms():
+        for j in range(nx):
+            product(nx + j, 512, 192, (0, 96, BOTTOMS + j * 96))
+
+    def far_products():
+        for j in range(nx):
+            product(nx + j, 0, 704, (0, 256, TOPS + j * 256), (512, 96, BOTTOMS + j * 96))
 
     def scatter(at, count, start, stop, first):
         got = jnp.dot(S[at : at + count, start:stop], PR[start:stop], preferred_element_type=f32)
@@ -296,47 +342,31 @@
         unpack_a(j, e)
         unpack_d(j, e)
         unpack_c(j, e)
-        near_products(j)
         return carry
 
+    def far(k, unpack):
+        cells = [cell_of(nx + j) for j in range(nx)]
+        for e in cells[1:]:
+            piece_copy(e, k, zpeer, z_send.at[k]).wait_recv()
+        for j, e in enumerate(cells):
+            unpack(nx + j, e)
+
     forward(0)
-    lax.fori_loop(0, 2, near_cell, 0)
-    forward(1)
-    lax.fori_loop(2, nx, near_cell, 0)
+    lax.fori_loop(0, nx, near_cell, 0)
+    near_products()
     for at in range(0, EXT, EXT // 2):
         scatter(at, EXT // 2, 0, TOPS, True)
-
-    def far(k, unpack):
-        def body(j, carry):
-            e = cell_of(nx + j)
-
-            @pl.when(j > 0)
-            def _():
-                piece_copy(e, k, zpeer, z_send.at[k]).wait_recv()
-
-            unpack(nx + j, e)
-            return carry
-
-        lax.fori_loop(0, nx, body, 0)
-
+    forward(1)
     far(0, unpack_b)
+    forward(2)
     far(1, unpack_a)
-    forward(2)
     forward(3)
     far(2, unpack_d)
-
-    def all_far(rows_of):
-        def body(j, carry):
-            rows_of(j)
-            return carry
-
-        lax.fori_loop(0, nx, body, 0)
-
-    all_far(far_tops)
+    far_tops()
     for at in range(0, EXT, EXT // 2):
         scatter(at, EXT // 2, TOPS, BOTTOMS, False)
     far(3, unpack_c)
-    all_far(far_bottoms)
+    far_bottoms()
     end = BOTTOMS + nx * 96
     scatter(LOW, 2 * FACE, BOTTOMS, end, False)
 
@@ -384,18 +414,8 @@
     set_first(HIGH + FACE, FACE, T[HIGH + FACE : EXT] + XR[1, FACE:], has_high)
     gather(EARLY, EXT, False)
 
-    def second_near(j, carry):
-        near_products(j)
-        return carry
-
-    lax.fori_loop(0, nx, second_near, 0)
-
-    def second_far(j, carry):
-        far_tops(j)
-        far_bottoms(j)
-        return carry
-
-    lax.fori_loop(0, nx, second_far, 0)
+    near_products()
+    far_products()
 
     @pl.when(has_low)
     def _():
@@ -417,12 +437,15 @@
     def _():
         own_up.start()
 
-    def finish(to, at, count, total):
-        value = (total - center * F[at : at + count]) * (2.0 / half)
-        out[to : to + count] = value - SX[at : at + count]
+    def finish(i, to, at, count, total):
+        O[to : to + count] = (total - center * F[at : at + count]) * (2.0 / half)
+        part = pl.ds(to, count)
+        store = pltpu.make_async_copy(O.at[part], out.at[part], local.at[i])
+        store.start()
+        return store
 
     scatter(0, INNER, 0, end, True)
-    finish(FACE, 0, INNER, T[0:INNER])
+    stores = [finish(0, FACE, 0, INNER, T[0:INNER])]
     scatter(LOW + FACE, 2 * FACE, 0, end, True)
 
     @pl.when(has_low)
@@ -441,8 +464,8 @@
     def _():
         YR[1] = jnp.zeros((FACE, COLS), f32)
 
-    finish(0, LOW + FACE, FACE, T[LOW + FACE : HIGH] + YR[0])
-    finish(OWN - FACE, HIGH, FACE, T[HIGH : HIGH + FACE] + YR[1])
+    stores.append(finish(1, 0, LOW + FACE, FACE, T[LOW + FACE : HIGH] + YR[0]))
+    stores.append(finish(2, OWN - FACE, HIGH, FACE, T[HIGH : HIGH + FACE] + YR[1]))
 
     for c in z_copies + x_copies:
         c.wait_send()
@@ -460,15 +483,18 @@
         halo_up.wait_send()
         own_up.wait_send()
 
+    for c in stores:
+        c.wait()
+
 
 def on_device(states, connectivity, cell_hamiltonian):
-    vmem = pl.BlockSpec(memory_space=pltpu.VMEM)
+    anywhere = pl.BlockSpec(memory_space=pl.ANY)
     kt = CELLS * KC
-    return pl.pallas_call(
+    moved = pl.pallas_call(
         kernel,
         out_shape=jax.ShapeDtypeStruct((OWN, COLS), f32),
-        in_specs=[vmem] * 3,
-        out_specs=vmem,
+        in_specs=[anywhere] * 3,
+        out_specs=anywhere,
         scratch_shapes=[
             pltpu.VMEM((kt, EXT), bf16),
             pltpu.VMEM((EXT, kt), bf16),
@@ -485,17 +511,22 @@
             pltpu.VMEM((KC, 384), f32),
             pltpu.VMEM((CELLS, 384), i32),
             pltpu.VMEM((1, kt), i32),
+            pltpu.VMEM((CELLS, NPC), i32),
+            pltpu.VMEM((NPC, 1, NPC), f32),
+            pltpu.VMEM((OWN, COLS), f32),
             pltpu.SemaphoreType.DMA((4,)),
             pltpu.SemaphoreType.DMA((3,)),
             pltpu.SemaphoreType.DMA((4, 3)),
             pltpu.SemaphoreType.DMA((6,)),
             pltpu.SemaphoreType.DMA((CELLS, 4)),
             pltpu.SemaphoreType.DMA((6,)),
+            pltpu.SemaphoreType.DMA((5,)),
         ],
         compiler_params=pltpu.CompilerParams(
             collective_id=0, has_side_effects=True, vmem_limit_bytes=58 << 20
         ),
-    )(states, connectivity, cell_hamiltonian)
+    )(states, connectivity, cell_hamiltonian.reshape(NPC, 1, NPC))
+    return moved - states
 
 
 def solution(mesh):

time: 86.4 us -> 77.7 us (0.90)
  Pallas kernels: 82.1 us -> 75.4 us
  local copies, waits for them, and re-layouts: 4.01 us -> 0.01 us
  other arithmetic: 0 us -> 2.17 us
    pallas_call x1, Pallas kernels: 82.1 us -> 75.4 us  [on_device(): pl.pallas_call(kernel, out_shape=jax.ShapeDtypeStruct((OWN, COLS), f32),...]
    unnamed x2, local copies, waits for them, and re-layouts: 4.01 us -> 0.01 us
    sub x0 -> x1, other arithmetic: none -> 2.17 us  [on_device(): return moved - states]
where the time goes in v2:
time: 77.7 us; the launch traced here: 77.6 us
  Pallas kernels  75.4 us (97%)
  other arithmetic  2.17 us (3%)
    pallas_call x1, Pallas kernels, on_device(): pl.pallas_call(kernel, out_shape=jax.ShapeDtypeStruct((OWN, COLS), f32),...  75.4 us
    sub x1, other arithmetic, on_device(): return moved - states  2.17 us

profile of v2, /device:TPU:32, one launch (start us, length us, event | category | flops | bytes accessed | tf_op | source)
XLA Modules:
  0.0 77.6 jit_solution(3736751905624990659)
XLA Ops:
  0.0 0.0 copy-start
  0.0 75.4 %shard_map.37 = f32[1728,128]{1,0:T(8,128)} custom-call(f32[1728,128]{1,0:T(8,128)} %states.1, s32[8,343]{1,0:T(8,128)} %conn.1, f32[343,1,343]{2,1,0:T(1,128)} %bitcast.1), custom_call_target="tpu_custom_call" | custom-call | tf_op jit(solution)/shard_map/pallas_call | solution.py:493
  75.4 0.0 copy-done
  75.4 2.2 %sub.3 = f32[1728,128]{1,0:T(8,128)} subtract(f32[1728,128]{1,0:T(8,128)} %shard_map.37, f32[1728,128]{1,0:T(8,128)S(1)} %copy-done) | non-fusion elementwise | flops 221184 | bytes 2654208 | tf_op jit(solution)/shard_map/sub | solution.py:529
Async XLA Ops:
  0.0 75.4 %copy-start = (f32[1728,128]{1,0:T(8,128)S(1)}, f32[1728,128]{1,0:T(8,128)}, u32[]{:S(2)}) copy-start(f32[1728,128]{1,0:T(8,128)} %states.1) | copy-start | bytes 2654212

commit v3 on v2

--- a/solution.py
+++ b/solution.py
@@ -23,8 +23,9 @@
 HIGH = INNER + 2 * FACE
 EARLY = 1024
 
-PB, PA, PD, PC, PROWS = 0, 176, 304, 432, 480
-PIECES = ((PB, 176), (PA, 128), (PD, 128), (PC, 48))
+PB, PA, PC, PD, PROWS = 0, 176, 304, 352, 480
+PIECES = ((0, 88), (88, 88), (176, 88), (264, 88), (352, 64), (416, 64))
+HOP = 4
 
 center = 0.5
 half = 1.5
@@ -73,7 +74,7 @@
 def kernel(
     states, conn, cell, out,
     G, S, Hs, X, PR, E, RX, T, SX, F, XR, YR, Hf, CP, CR, CN, V, O,
-    z_send, x_send, f_send, n_send, cell_recv, n_recv, local,
+    RL, z_send, z_recv, x_send, f_send, n_send, cell_recv, n_recv, local,
 ):
     d = lax.axis_index("domain")
     b = lax.axis_index("band")
@@ -83,6 +84,12 @@
     zh = b % 2
     zpeer = 2 * xi + 1 - zh
     xpeers = [2 * ((xi + j) % nx) + zh for j in (1, 3, 2)]
+    z = 8 * zh + d // 8
+
+    def along_z(way):
+        to = (z + (HOP, 16 - HOP)[way]) % 16
+        return (to % 8) * 8 + d % 8, 2 * xi + to // 8, to // 8
+
     has_low = d > 0
     has_high = d < last
 
@@ -91,7 +98,8 @@
     def greet(dd, bb):
         pl.semaphore_signal(barrier, inc=1, device_id=(dd, bb), device_id_type=MESH)
 
-    greet(d, zpeer)
+    for way in range(2):
+        greet(*along_z(way)[:2])
     for p in xpeers:
         greet(d, p)
 
@@ -127,11 +135,10 @@
     RX[b, PD : PD + 128] = jnp.where(row >= col, Hf[0:128, 0:128], d2)
     RX[b, PC : PC + 48] = pack_corner(Hf[256:344, 256:384], lane_roll)
 
-    pl.semaphore_wait(barrier, 4 + has_low.astype(i32) + has_high.astype(i32))
+    pl.semaphore_wait(barrier, 5 + has_low.astype(i32) + has_high.astype(i32))
 
     def piece_copy(e, k, target, send_sem):
-        at, rows = PIECES[k]
-        part = RX.at[e, pl.ds(at, rows)]
+        part = RX.at[e, pl.ds(*PIECES[k])]
         return pltpu.make_async_remote_copy(
             src_ref=part, dst_ref=part, send_sem=send_sem, recv_sem=cell_recv.at[e, k],
             device_id=(d, target), device_id_type=MESH,
@@ -149,9 +156,18 @@
             device_id=(dd, b), device_id_type=MESH,
         )
 
-    z_copies = [piece_copy(b, k, zpeer, z_send.at[k]) for k in range(4)]
-    for c in z_copies:
-        c.start()
+    def z_copy(leg, k):
+        dd, bb, side = along_z(k % 2)
+        rows = pl.ds(*PIECES[k])
+        return pltpu.make_async_remote_copy(
+            src_ref=RL.at[rows] if leg else RX.at[b, rows],
+            dst_ref=RX.at[2 * xi + 1 - side, rows] if leg else RL.at[rows],
+            send_sem=z_send.at[leg, k], recv_sem=z_recv.at[leg, k],
+            device_id=(dd, bb), device_id_type=MESH,
+        )
+
+    for k in range(4):
+        z_copy(0, k).start()
     x_copies = [whole_copy(b, p, x_send.at[j]) for j, p in enumerate(xpeers)]
     for c in x_copies:
         c.start()
@@ -249,23 +265,30 @@
 
     half_rows = CELLS * KC // 2
 
+    def gather_half(m, start, stop, first):
+        r = pl.ds(pl.multiple_of(m * half_rows, half_rows), half_rows)
+        got = jnp.dot(G[r, start:stop], E[start:stop], preferred_element_type=f32)
+        if not first:
+            got = got + X[r, :].astype(f32)
+        X[r, :] = got.astype(bf16)
+
     def gather(start, stop, first):
         def body(m, carry):
-            r = pl.ds(pl.multiple_of(m * half_rows, half_rows), half_rows)
-            got = jnp.dot(G[r, start:stop], E[start:stop], preferred_element_type=f32)
-            if not first:
-                got = got + X[r, :].astype(f32)
-            X[r, :] = got.astype(bf16)
+            gather_half(m, start, stop, first)
             return carry
 
         lax.fori_loop(0, 2, body, 0)
 
-    gather(0, EXT, True)
-
-    def forward(k):
-        piece_copy(zpeer, k, zpeer, z_send.at[k]).wait_recv()
-        for j, p in enumerate(xpeers):
-            piece_copy(zpeer, k, p, f_send.at[k, j]).start()
+    def relay(group):
+        for k in (2 * group, 2 * group + 1):
+            z_copy(0, k).wait_recv()
+            z_copy(1, k).start()
+
+    def forward(group):
+        for k in (2 * group, 2 * group + 1):
+            z_copy(1, k).wait_recv()
+            for j, p in enumerate(xpeers):
+                piece_copy(zpeer, k, p, f_send.at[k, j]).start()
 
     def put(s, at, count, lane, value):
         hi, lo = split(value)
@@ -327,9 +350,10 @@
             product(nx + j, 0, 704, (0, 256, TOPS + j * 256), (512, 96, BOTTOMS + j * 96))
 
     def scatter(at, count, start, stop, first):
-        got = jnp.dot(S[at : at + count, start:stop], PR[start:stop], preferred_element_type=f32)
+        w = pl.ds(at, count)
+        got = jnp.dot(S[w, start:stop], PR[start:stop], preferred_element_type=f32)
         got = got[:, :COLS] + got[:, COLS:]
-        T[at : at + count] = got if first else T[at : at + count] + got
+        T[w, :] = got if first else T[w, :] + got
 
     def near_cell(j, carry):
         e = cell_of(j)
@@ -344,74 +368,101 @@
         unpack_c(j, e)
         return carry
 
-    def far(k, unpack):
-        cells = [cell_of(nx + j) for j in range(nx)]
-        for e in cells[1:]:
-            piece_copy(e, k, zpeer, z_send.at[k]).wait_recv()
-        for j, e in enumerate(cells):
-            unpack(nx + j, e)
-
-    forward(0)
+    far_cells = [cell_of(nx + j) for j in range(nx)]
+
+    def arrived(group):
+        for e in far_cells[1:]:
+            for k in (2 * group, 2 * group + 1):
+                piece_copy(e, k, zpeer, z_send.at[0, k]).wait_recv()
+
+    core = d % 2
+    down_first = core == 0
+
+    def start_both(down, up):
+        def begin(place):
+            @pl.when(has_low & (down_first if place == 0 else jnp.logical_not(down_first)))
+            def _():
+                down.start()
+
+            @pl.when(has_high & (jnp.logical_not(down_first) if place == 0 else down_first))
+            def _():
+                up.start()
+
+        return begin
+
+    end = BOTTOMS + nx * 96
+
+    gather_half(0, 0, EXT, True)
+    relay(0)
+    z_copy(0, 4).start()
+    z_copy(0, 5).start()
+    gather_half(1, 0, EXT, True)
     lax.fori_loop(0, nx, near_cell, 0)
     near_products()
+    relay(1)
+    scatter(0, EXT // 2, 0, TOPS, True)
+    forward(0)
+    scatter(EXT // 2, EXT // 2, 0, TOPS, True)
+    relay(2)
+    arrived(0)
+    for j, e in enumerate(far_cells):
+        unpack_b(nx + j, e)
+    forward(1)
+    arrived(1)
+    for j, e in enumerate(far_cells):
+        unpack_a(nx + j, e)
+        unpack_c(nx + j, e)
+    far_bottoms()
+    forward(2)
     for at in range(0, EXT, EXT // 2):
-        scatter(at, EXT // 2, 0, TOPS, True)
-    forward(1)
-    far(0, unpack_b)
-    forward(2)
-    far(1, unpack_a)
-    forward(3)
-    far(2, unpack_d)
+        scatter(at, EXT // 2, BOTTOMS, end, False)
+    arrived(2)
+    for j, e in enumerate(far_cells):
+        unpack_d(nx + j, e)
     far_tops()
-    for at in range(0, EXT, EXT // 2):
-        scatter(at, EXT // 2, TOPS, BOTTOMS, False)
-    far(3, unpack_c)
-    far_bottoms()
-    end = BOTTOMS + nx * 96
-    scatter(LOW, 2 * FACE, BOTTOMS, end, False)
-
-    @pl.when(has_low)
-    def _():
-        sum_down.start()
-
-    scatter(HIGH, 2 * FACE, BOTTOMS, end, False)
-
-    @pl.when(has_high)
-    def _():
-        sum_up.start()
-
-    scatter(0, INNER, BOTTOMS, end, False)
-
-    def set_first(at, count, total, keep=None):
-        value = (total - center * SX[at : at + count]) * (1.0 / half)
-        if keep is not None:
-            value = jnp.where(keep, value, 0.0)
-        F[at : at + count] = value
-        set_field(at, count, value)
-
-    set_first(0, INNER, T[0:INNER])
+    begin_sums = start_both(sum_down, sum_up)
+    for place in range(2):
+        region = core if place == 0 else 1 - core
+        scatter(pl.multiple_of(LOW + 2 * FACE * region, 2 * FACE), 2 * FACE, TOPS, BOTTOMS, False)
+        begin_sums(place)
+    scatter(0, INNER, TOPS, BOTTOMS, False)
+
+    def keep_field(at, count, value):
+        w = pl.ds(at, count)
+        F[w, :] = value
+        hi, lo = split(value)
+        E[w, 0:COLS] = hi
+        E[w, COLS : 2 * COLS] = lo
+
+    def as_first(total, at, count):
+        return (total - center * SX[pl.ds(at, count), :]) * (1.0 / half)
+
+    keep_field(0, INNER, as_first(T[0:INNER], 0, INNER))
     gather(0, EARLY, True)
 
-    @pl.when(has_low)
-    def _():
-        sum_up.wait_recv()
-
-    @pl.when(jnp.logical_not(has_low))
-    def _():
-        XR[0] = jnp.zeros((2 * FACE, COLS), f32)
-
-    @pl.when(has_high)
-    def _():
-        sum_down.wait_recv()
-
-    @pl.when(jnp.logical_not(has_high))
-    def _():
-        XR[1] = jnp.zeros((2 * FACE, COLS), f32)
-
-    set_first(LOW, FACE, T[LOW : LOW + FACE] + XR[0, 0:FACE], has_low)
-    set_first(LOW + FACE, FACE, T[LOW + FACE : HIGH] + XR[0, FACE:])
-    set_first(HIGH, FACE, T[HIGH : HIGH + FACE] + XR[1, 0:FACE])
-    set_first(HIGH + FACE, FACE, T[HIGH + FACE : EXT] + XR[1, FACE:], has_high)
+    def wait_for(region, from_low, from_high, buffer):
+        low, high = region == 0, region == 1
+
+        @pl.when(low & has_low)
+        def _():
+            from_low.wait_recv()
+
+        @pl.when(high & has_high)
+        def _():
+            from_high.wait_recv()
+
+        @pl.when((low & jnp.logical_not(has_low)) | (high & jnp.logical_not(has_high)))
+        def _():
+            buffer[region] = jnp.zeros(buffer.shape[1:], f32)
+
+    for place in range(2):
+        region = 1 - core if place == 0 else core
+        wait_for(region, sum_up, sum_down, XR)
+        for part in range(2):
+            at = pl.multiple_of(LOW + 2 * FACE * region + FACE * part, FACE)
+            total = T[pl.ds(at, FACE), :] + XR[region, FACE * part : FACE * (part + 1)]
+            inside = (region == 1) | has_low if part == 0 else (region == 0) | has_high
+            keep_field(at, FACE, jnp.where(inside, as_first(total, at, FACE), 0.0))
     gather(EARLY, EXT, False)
 
     near_products()
@@ -425,21 +476,15 @@
     def _():
         sum_up.wait_send()
 
-    scatter(LOW, FACE, 0, end, True)
-
-    @pl.when(has_low)
-    def _():
-        own_down.start()
-
-    scatter(HIGH + FACE, FACE, 0, end, True)
-
-    @pl.when(has_high)
-    def _():
-        own_up.start()
+    begin_owned = start_both(own_down, own_up)
+    for place in range(2):
+        region = core if place == 0 else 1 - core
+        scatter(pl.multiple_of(LOW + 3 * FACE * region, FACE), FACE, 0, end, True)
+        begin_owned(place)
 
     def finish(i, to, at, count, total):
-        O[to : to + count] = (total - center * F[at : at + count]) * (2.0 / half)
         part = pl.ds(to, count)
+        O[part, :] = (total - center * F[pl.ds(at, count), :]) * (2.0 / half)
         store = pltpu.make_async_copy(O.at[part], out.at[part], local.at[i])
         store.start()
         return store
@@ -447,29 +492,18 @@
     scatter(0, INNER, 0, end, True)
     stores = [finish(0, FACE, 0, INNER, T[0:INNER])]
     scatter(LOW + FACE, 2 * FACE, 0, end, True)
-
-    @pl.when(has_low)
-    def _():
-        own_up.wait_recv()
-
-    @pl.when(jnp.logical_not(has_low))
-    def _():
-        YR[0] = jnp.zeros((FACE, COLS), f32)
-
-    @pl.when(has_high)
-    def _():
-        own_down.wait_recv()
-
-    @pl.when(jnp.logical_not(has_high))
-    def _():
-        YR[1] = jnp.zeros((FACE, COLS), f32)
-
-    stores.append(finish(1, 0, LOW + FACE, FACE, T[LOW + FACE : HIGH] + YR[0]))
-    stores.append(finish(2, OWN - FACE, HIGH, FACE, T[HIGH : HIGH + FACE] + YR[1]))
-
-    for c in z_copies + x_copies:
+    for place in range(2):
+        region = 1 - core if place == 0 else core
+        wait_for(region, own_up, own_down, YR)
+        at = pl.multiple_of(LOW + FACE + FACE * region, FACE)
+        to = pl.multiple_of((OWN - FACE) * region, FACE)
+        stores.append(finish(1 + place, to, at, FACE, T[pl.ds(at, FACE), :] + YR[region]))
+
+    for c in x_copies:
         c.wait_send()
-    for k in range(4):
+    for k in range(len(PIECES)):
+        z_copy(0, k).wait_send()
+        z_copy(1, k).wait_send()
         for j, p in enumerate(xpeers):
             piece_copy(zpeer, k, p, f_send.at[k, j]).wait_send()
 
@@ -514,11 +548,13 @@
             pltpu.VMEM((CELLS, NPC), i32),
             pltpu.VMEM((NPC, 1, NPC), f32),
             pltpu.VMEM((OWN, COLS), f32),
-            pltpu.SemaphoreType.DMA((4,)),
+            pltpu.VMEM((PROWS, 128), f32),
+            pltpu.SemaphoreType.DMA((2, 6)),
+            pltpu.SemaphoreType.DMA((2, 6)),
             pltpu.SemaphoreType.DMA((3,)),
-            pltpu.SemaphoreType.DMA((4, 3)),
+            pltpu.SemaphoreType.DMA((6, 3)),
             pltpu.SemaphoreType.DMA((6,)),
-            pltpu.SemaphoreType.DMA((CELLS, 4)),
+            pltpu.SemaphoreType.DMA((CELLS, 6)),
             pltpu.SemaphoreType.DMA((6,)),
             pltpu.SemaphoreType.DMA((5,)),
         ],

time: 77.7 us -> 73.6 us (0.947)
  the two profiles are of different devices: /device:TPU:32 before, /device:TPU:25 now
where the time goes in v3:
time: 73.6 us; the launch traced here: 72.6 us
  Pallas kernels  70.4 us (96%)
  other arithmetic  2.17 us (3%)
    pallas_call x1, Pallas kernels, on_device(): pl.pallas_call(kernel, out_shape=jax.ShapeDtypeStruct((OWN, COLS), f32),...  70.4 us
    sub x1, other arithmetic, on_device(): return moved - states  2.17 us

profile of v3, /device:TPU:25, one launch (start us, length us, event | category | flops | bytes accessed | tf_op | source)
XLA Modules:
  0.0 72.6 jit_solution(4735902745094816377)
XLA Ops:
  0.0 0.0 copy-start
  0.0 70.4 %shard_map.37 = f32[1728,128]{1,0:T(8,128)} custom-call(f32[1728,128]{1,0:T(8,128)} %states.1, s32[8,343]{1,0:T(8,128)} %conn.1, f32[343,1,343]{2,1,0:T(1,128)} %bitcast.1), custom_call_target="tpu_custom_call" | custom-call | tf_op jit(solution)/shard_map/pallas_call | solution.py:527
  70.4 0.0 copy-done
  70.4 2.2 %sub.3 = f32[1728,128]{1,0:T(8,128)} subtract(f32[1728,128]{1,0:T(8,128)} %shard_map.37, f32[1728,128]{1,0:T(8,128)S(1)} %copy-done) | non-fusion elementwise | flops 221184 | bytes 2654208 | tf_op jit(solution)/shard_map/sub | solution.py:565
Async XLA Ops:
  0.0 70.4 %copy-start = (f32[1728,128]{1,0:T(8,128)S(1)}, f32[1728,128]{1,0:T(8,128)}, u32[]{:S(2)}) copy-start(f32[1728,128]{1,0:T(8,128)} %states.1) | copy-start | bytes 2654212

commit v4 on v3

--- a/solution.py
+++ b/solution.py
@@ -392,28 +392,28 @@
 
     end = BOTTOMS + nx * 96
 
-    gather_half(0, 0, EXT, True)
     relay(0)
     z_copy(0, 4).start()
     z_copy(0, 5).start()
+    gather_half(0, 0, EXT, True)
     gather_half(1, 0, EXT, True)
+    relay(1)
     lax.fori_loop(0, nx, near_cell, 0)
     near_products()
-    relay(1)
-    scatter(0, EXT // 2, 0, TOPS, True)
     forward(0)
-    scatter(EXT // 2, EXT // 2, 0, TOPS, True)
     relay(2)
+    for at in range(0, EXT, EXT // 2):
+        scatter(at, EXT // 2, 0, TOPS, True)
+    forward(1)
+    forward(2)
     arrived(0)
     for j, e in enumerate(far_cells):
         unpack_b(nx + j, e)
-    forward(1)
     arrived(1)
     for j, e in enumerate(far_cells):
         unpack_a(nx + j, e)
         unpack_c(nx + j, e)
     far_bottoms()
-    forward(2)
     for at in range(0, EXT, EXT // 2):
         scatter(at, EXT // 2, BOTTOMS, end, False)
     arrived(2)

time: 73.6 us -> 67.6 us (0.918)
  Pallas kernels: 70.4 us -> 64.8 us
    pallas_call x1, Pallas kernels: 70.4 us -> 64.8 us  [on_device(): pl.pallas_call(kernel, out_shape=jax.ShapeDtypeStruct((OWN, COLS), f32),...]
where the time goes in v4:
time: 67.6 us; the launch traced here: 67 us
  Pallas kernels  64.8 us (96%)
  other arithmetic  2.17 us (3%)
    pallas_call x1, Pallas kernels, on_device(): pl.pallas_call(kernel, out_shape=jax.ShapeDtypeStruct((OWN, COLS), f32),...  64.8 us
    sub x1, other arithmetic, on_device(): return moved - states  2.17 us

profile of v4, /device:TPU:25, one launch (start us, length us, event | category | flops | bytes accessed | tf_op | source)
XLA Modules:
  0.0 67.0 jit_solution(6485437447721198215)
XLA Ops:
  0.0 0.0 copy-start
  0.0 64.8 %shard_map.37 = f32[1728,128]{1,0:T(8,128)} custom-call(f32[1728,128]{1,0:T(8,128)} %states.1, s32[8,343]{1,0:T(8,128)} %conn.1, f32[343,1,343]{2,1,0:T(1,128)} %bitcast.1), custom_call_target="tpu_custom_call" | custom-call | tf_op jit(solution)/shard_map/pallas_call | solution.py:527
  64.9 0.0 copy-done
  64.9 2.2 %sub.3 = f32[1728,128]{1,0:T(8,128)} subtract(f32[1728,128]{1,0:T(8,128)} %shard_map.37, f32[1728,128]{1,0:T(8,128)S(1)} %copy-done) | non-fusion elementwise | flops 221184 | bytes 2654208 | tf_op jit(solution)/shard_map/sub | solution.py:565
Async XLA Ops:
  0.0 64.9 %copy-start = (f32[1728,128]{1,0:T(8,128)S(1)}, f32[1728,128]{1,0:T(8,128)}, u32[]{:S(2)}) copy-start(f32[1728,128]{1,0:T(8,128)} %states.1) | copy-start | bytes 2654212

commit v5 on v4

--- a/solution.py
+++ b/solution.py
@@ -73,7 +73,7 @@
 
 def kernel(
     states, conn, cell, out,
-    G, S, Hs, X, PR, E, RX, T, SX, F, XR, YR, Hf, CP, CR, CN, V, O,
+    G, S, Hs, X, PR, E, RX, T, SX, F, XR, YR, Hf, CP, CR, CN, V,
     RL, z_send, z_recv, x_send, f_send, n_send, cell_recv, n_recv, local,
 ):
     d = lax.axis_index("domain")
@@ -83,7 +83,7 @@
     xi = b // 2
     zh = b % 2
     zpeer = 2 * xi + 1 - zh
-    xpeers = [2 * ((xi + j) % nx) + zh for j in (1, 3, 2)]
+    xpeers = [2 * ((xi + j) % nx) + zh for j in (2, 1, 3)]
     z = 8 * zh + d // 8
 
     def along_z(way):
@@ -484,20 +484,17 @@
 
     def finish(i, to, at, count, total):
         part = pl.ds(to, count)
-        O[part, :] = (total - center * F[pl.ds(at, count), :]) * (2.0 / half)
-        store = pltpu.make_async_copy(O.at[part], out.at[part], local.at[i])
-        store.start()
-        return store
+        out[part, :] = (total - center * F[pl.ds(at, count), :]) * (2.0 / half)
 
     scatter(0, INNER, 0, end, True)
-    stores = [finish(0, FACE, 0, INNER, T[0:INNER])]
+    finish(0, FACE, 0, INNER, T[0:INNER])
     scatter(LOW + FACE, 2 * FACE, 0, end, True)
     for place in range(2):
         region = 1 - core if place == 0 else core
         wait_for(region, own_up, own_down, YR)
         at = pl.multiple_of(LOW + FACE + FACE * region, FACE)
         to = pl.multiple_of((OWN - FACE) * region, FACE)
-        stores.append(finish(1 + place, to, at, FACE, T[pl.ds(at, FACE), :] + YR[region]))
+        finish(1 + place, to, at, FACE, T[pl.ds(at, FACE), :] + YR[region])
 
     for c in x_copies:
         c.wait_send()
@@ -517,18 +514,15 @@
         halo_up.wait_send()
         own_up.wait_send()
 
-    for c in stores:
-        c.wait()
-
 
 def on_device(states, connectivity, cell_hamiltonian):
     anywhere = pl.BlockSpec(memory_space=pl.ANY)
     kt = CELLS * KC
     moved = pl.pallas_call(
         kernel,
-        out_shape=jax.ShapeDtypeStruct((OWN, COLS), f32),
+        out_shape=pltpu.VMEM((OWN, COLS), f32),
         in_specs=[anywhere] * 3,
-        out_specs=anywhere,
+        out_specs=pl.BlockSpec(memory_space=pltpu.VMEM),
         scratch_shapes=[
             pltpu.VMEM((kt, EXT), bf16),
             pltpu.VMEM((EXT, kt), bf16),
@@ -547,7 +541,6 @@
             pltpu.VMEM((1, kt), i32),
             pltpu.VMEM((CELLS, NPC), i32),
             pltpu.VMEM((NPC, 1, NPC), f32),
-            pltpu.VMEM((OWN, COLS), f32),
             pltpu.VMEM((PROWS, 128), f32),
             pltpu.SemaphoreType.DMA((2, 6)),
             pltpu.SemaphoreType.DMA((2, 6)),

time: 67.6 us -> 65.5 us (0.969)
  other arithmetic: 2.17 us -> 1 us
  Pallas kernels: 64.8 us -> 64.1 us
    sub x1, other arithmetic: 2.17 us -> 1 us  [on_device(): return moved - states]
    pallas_call x1, Pallas kernels: 64.8 us -> 64.1 us  [on_device(): pl.pallas_call(kernel, out_shape=pltpu.VMEM((OWN, COLS), f32), in_specs=[...]
where the time goes in v5:
time: 65.5 us; the launch traced here: 65.1 us
  Pallas kernels  64.1 us (98%)
  other arithmetic  1 us (2%)
    pallas_call x1, Pallas kernels, on_device(): pl.pallas_call(kernel, out_shape=pltpu.VMEM((OWN, COLS), f32), in_specs=[...  64.1 us

profile of v5, /device:TPU:25, one launch (start us, length us, event | category | flops | bytes accessed | tf_op | source)
XLA Modules:
  0.0 65.1 jit_solution(7410532313370488274)
XLA Ops:
  0.0 0.0 copy-start
  0.0 64.1 %shard_map.37 = f32[1728,128]{1,0:T(8,128)S(1)} custom-call(f32[1728,128]{1,0:T(8,128)} %states.1, s32[8,343]{1,0:T(8,128)} %conn.1, f32[343,1,343]{2,1,0:T(1,128)} %bitcast.1), custom_call_target="tpu_custom_call" | custom-call | tf_op jit(solution)/shard_map/pallas_call | solution.py:521
  64.1 0.0 copy-done
  64.1 1.0 %sub.3 = f32[1728,128]{1,0:T(8,128)} subtract(f32[1728,128]{1,0:T(8,128)S(1)} %shard_map.37, f32[1728,128]{1,0:T(8,128)S(1)} %copy-done) | non-fusion elementwise | flops 221184 | bytes 2654208 | tf_op jit(solution)/shard_map/sub | solution.py:558
Async XLA Ops:
  0.0 64.1 %copy-start = (f32[1728,128]{1,0:T(8,128)S(1)}, f32[1728,128]{1,0:T(8,128)}, u32[]{:S(2)}) copy-start(f32[1728,128]{1,0:T(8,128)} %states.1) | copy-start | bytes 2654212

commit v6 on v5

--- a/solution.py
+++ b/solution.py
@@ -337,8 +337,8 @@
         for j in range(nx):
             product(j, 0, 704, (0, 256, j * KC), (512, 96, j * KC + 256))
 
-    def far_tops():
-        for j in range(nx):
+    def far_tops(some):
+        for j in some:
             product(nx + j, 0, 512, (0, 256, TOPS + j * 256))
 
     def far_bottoms():
@@ -416,10 +416,14 @@
     far_bottoms()
     for at in range(0, EXT, EXT // 2):
         scatter(at, EXT // 2, BOTTOMS, end, False)
-    arrived(2)
-    for j, e in enumerate(far_cells):
-        unpack_d(nx + j, e)
-    far_tops()
+    for some in ((0,), (1, 3), (2,)):
+        for j in some:
+            if j > 0:
+                for k in (4, 5):
+                    piece_copy(far_cells[j], k, zpeer, z_send.at[0, k]).wait_recv()
+        for j in some:
+            unpack_d(nx + j, far_cells[j])
+        far_tops(some)
     begin_sums = start_both(sum_down, sum_up)
     for place in range(2):
         region = core if place == 0 else 1 - core

time: 65.5 us -> 65.6 us (level)
  no operation moved by 1% of the time
where the time goes in v6:
time: 65.6 us; the launch traced here: 65.5 us
  Pallas kernels  64.5 us (98%)
  other arithmetic  1 us (2%)
    pallas_call x1, Pallas kernels, on_device(): pl.pallas_call(kernel, out_shape=pltpu.VMEM((OWN, COLS), f32), in_specs=[...  64.5 us

profile of v6, /device:TPU:25, one launch (start us, length us, event | category | flops | bytes accessed | tf_op | source)
XLA Modules:
  0.0 65.5 jit_solution(1670711806673985091)
XLA Ops:
  0.0 0.0 copy-start
  0.0 64.5 %shard_map.37 = f32[1728,128]{1,0:T(8,128)S(1)} custom-call(f32[1728,128]{1,0:T(8,128)} %states.1, s32[8,343]{1,0:T(8,128)} %conn.1, f32[343,1,343]{2,1,0:T(1,128)} %bitcast.1), custom_call_target="tpu_custom_call" | custom-call | tf_op jit(solution)/shard_map/pallas_call | solution.py:525
  64.5 0.0 copy-done
  64.5 1.0 %sub.3 = f32[1728,128]{1,0:T(8,128)} subtract(f32[1728,128]{1,0:T(8,128)S(1)} %shard_map.37, f32[1728,128]{1,0:T(8,128)S(1)} %copy-done) | non-fusion elementwise | flops 221184 | bytes 2654208 | tf_op jit(solution)/shard_map/sub | solution.py:562
Async XLA Ops:
  0.0 64.5 %copy-start = (f32[1728,128]{1,0:T(8,128)S(1)}, f32[1728,128]{1,0:T(8,128)}, u32[]{:S(2)}) copy-start(f32[1728,128]{1,0:T(8,128)} %states.1) | copy-start | bytes 2654212
